TPU v7x, 32 devices: a whole 2x2x4 slice. The times are simulated.
32 devices in a mesh: pipe: 2 (over y), seq: 4 (over z), tensor: 4 (over x, core).
Axes of the slice: x: 2, y: 2, z: 4, core: 2. Of those that a mesh axis runs over, the one named last changes fastest.
Arguments:
- resid: bfloat16 [2, 2, 1024, 8192], P('pipe', None, 'seq', 'tensor'), may hold values from -16 to 16
- streams: bfloat16 [2, 2, 1024, 3, 8192], P('pipe', None, 'seq', None, 'tensor'), may hold values from -6 to 6
- filt: bfloat16 [7, 8192], P(None, 'tensor'), may hold values from -2 to 2
- q_gain: float32 [4096], P('tensor'), may hold values from 0.5 to 2
- k_gain: float32 [4096], P('tensor'), may hold values from 0.1 to 1.9
- out_weight: bfloat16 [4096, 8192], P('seq', 'tensor'), may hold values from -0.09375 to 0.09375
- contig_lengths: int32 [2, 4], replicated, may hold values from 1 to 512, 1024 in all within a row
Outputs:
- activations: bfloat16 [2, 2, 1024, 8192], P('pipe', None, 'seq', 'tensor')
Inputs may be any that keep to these rules, and one draw needn't show every extreme that they name: `contig_lengths`: each micro-batch's contigs lie end to end in order and fill its 1024 tokens; in every micro-batch the longest is exactly 512 tokens.
All inputs are finite; a program needn't handle non-finite values.
Results may differ from a plain program's by a relative error of at most 0.0062.
Values may be sent and summed in bfloat16 or wider, within the bound.
A program may use at most 128 MiB of HBM per device.

v0:
```python
import jax
import jax.numpy as jnp
from jax import lax
from jax.sharding import PartitionSpec as P

HD = 128


NEG_FILL = -1e30


def from_behind(value, axis, steps):
    count = lax.axis_size(axis)
    first, last = (max(0, -steps), min(count, count - steps))
    return lax.ppermute(value, axis, [(source, source + steps) for source in range(first, last)])


def segment_of(contig_ends, positions):
    return jnp.sum((contig_ends[:, None, :] <= positions[None, :, None]).astype(jnp.int32), axis=2)


def per_device(resid, streams, filt, q_gain, k_gain, out_weight, contig_lengths):
    resid_own = resid[0]
    streams_own = streams[0]
    tap_count = filt.shape[0]
    batch_count = resid_own.shape[0]
    tok_rows = resid_own.shape[1]
    local_heads = q_gain.shape[0] // HD
    attend_width = local_heads * HD
    section_index = lax.axis_index("pipe")
    seq_index = lax.axis_index("seq")
    gated = (
        streams_own[:, :, 0].astype(jnp.float32) * streams_own[:, :, 2].astype(jnp.float32)
    ).astype(jnp.bfloat16)
    prev_rows = from_behind(gated[:, tok_rows - (tap_count - 1) :], "seq", 1)

    def run_hyena(operand):
        extended = jnp.concatenate([prev_rows, gated], axis=1)
        conv_out = jnp.zeros(resid_own.shape, jnp.float32)
        for offset in range(tap_count):
            begin = tap_count - 1 - offset
            conv_out = conv_out + filt[offset].astype(jnp.float32) * extended[
                :, begin : begin + tok_rows
            ].astype(jnp.float32)
        return (
            resid_own.astype(jnp.float32) + streams_own[:, :, 1].astype(jnp.float32) * conv_out
        ).astype(jnp.bfloat16)

    def no_hyena(operand):
        return jnp.zeros_like(resid_own)

    hidden = lax.cond(section_index == 0, run_hyena, no_hyena, 0)
    attend = hidden.reshape(batch_count, tok_rows, local_heads, 2, HD)[:, :, :, 0].reshape(
        batch_count, tok_rows, attend_width
    )
    arrived = from_behind(attend, "pipe", 1)
    contig_ends = jnp.cumsum(contig_lengths, axis=1)
    reach_span = min(4, lax.axis_size("seq") // 2)
    pieces = [arrived]
    for distance in range(1, reach_span + 1):
        pieces.insert(0, from_behind(arrived, "seq", distance))
    key_source = jnp.concatenate(pieces, axis=1)
    key_rows = (reach_span + 1) * tok_rows

    def run_attention(operand):
        query_pos = seq_index * tok_rows + jnp.arange(tok_rows, dtype=jnp.int32)
        key_pos = (seq_index - reach_span) * tok_rows + jnp.arange(key_rows, dtype=jnp.int32)
        same = (
            segment_of(contig_ends, query_pos)[:, :, None]
            == segment_of(contig_ends, key_pos)[:, None, :]
        )
        causal = (key_pos[None, None, :] <= query_pos[None, :, None]) & (
            key_pos[None, None, :] >= 0
        )
        visible = same & causal
        queries = (
            (arrived.astype(jnp.float32) * q_gain)
            .astype(jnp.bfloat16)
            .reshape(batch_count, tok_rows, local_heads, HD)
        )
        keys = (
            (key_source.astype(jnp.float32) * k_gain)
            .astype(jnp.bfloat16)
            .reshape(batch_count, key_rows, local_heads, HD)
        )
        values = key_source.reshape(batch_count, key_rows, local_heads, HD)

        def one_batch(items):
            query_part, key_part, value_part, visible_part = items
            scores = (
                jnp.einsum("thd,shd->hts", query_part, key_part, preferred_element_type=jnp.float32)
                / HD
            )
            scores = jnp.where(visible_part[None], scores, NEG_FILL)
            top = jnp.max(scores, axis=-1, keepdims=True)
            weights = jnp.where(visible_part[None], jnp.exp(scores - top), 0.0)
            total = jnp.sum(weights, axis=-1)
            mixed = jnp.einsum(
                "hts,shd->thd",
                weights.astype(jnp.bfloat16),
                value_part,
                preferred_element_type=jnp.float32,
            )
            mixed = mixed / jnp.transpose(total)[..., None]
            return mixed.astype(jnp.bfloat16).reshape(tok_rows, attend_width)

        return lax.map(one_batch, (queries, keys, values, visible))

    def no_attention(operand):
        return jnp.zeros_like(arrived)

    mixed = lax.cond(section_index == 1, run_attention, no_attention, 0)
    all_heads = lax.all_gather(mixed, "tensor", axis=2, tiled=True)
    flattened = all_heads.reshape(batch_count * tok_rows, all_heads.shape[2])
    projected = jnp.dot(
        flattened,
        lax.all_gather(out_weight, "seq", axis=0, tiled=True),
        preferred_element_type=jnp.float32,
    )
    attn_out = projected.astype(jnp.bfloat16).reshape(batch_count, tok_rows, out_weight.shape[1])
    output = jnp.where(section_index == 0, hidden, attn_out)
    return output[None]


def solution(mesh):
    placed = (
        P("pipe", None, "seq", "tensor"),
        P("pipe", None, "seq", None, "tensor"),
        P(None, "tensor"),
        P("tensor"),
        P("tensor"),
        P("seq", "tensor"),
        P(),
    )
    return jax.shard_map(
        per_device,
        mesh=mesh,
        in_specs=placed,
        out_specs=P("pipe", None, "seq", "tensor"),
        check_vma=False,
    )
```

profile of v0, /device:TPU:13, one launch (start us, length us, event | category | flops | bytes accessed | tf_op | source)
XLA Modules:
  0.0 504.3 jit_solution(7723232726471942365)
XLA Ops:
  6.5 3.4 copy.31
  9.9 2.6 copy-done
  12.6 2.1 fusion.40
  14.7 0.9 slice.70
  15.6 3.2 collective-permute-start
  18.8 1.8 collective-permute-done
  20.9 3.0 reshape.143
  23.9 5.8 %copy.29 = bf16[2,256,8,1,128]{1,4,2,0,3:T(8,128)(2,1)} copy(bf16[2,256,8,1,128]{4,3,2,1,0:T(2,128)(2,1)} %bitcast.79) | data formatting | bytes 2097152
  29.7 1.3 collective-permute-start.1
  31.0 32.8 %collective-permute-done.1 = bf16[2,256,1024]{1,2,0:T(8,128)(2,1)S(1)} collective-permute-done((bf16[2,256,1024]{1,2,0:T(8,128)(2,1)}, bf16[2,256,1024]{1,2,0:T(8,128)(2,1)S(1)}, u32[]{:S(2)}, u32[]{:S(2)}) %collective-permute-start.1) | collective-permute-done | bytes 1048608 | tf_op jit(solution)/shard_map/ppermute | solution.py:15
  63.8 5.2 %collective-permute-start.2 = (bf16[2,256,1024]{1,2,0:T(8,128)(2,1)S(1)}, bf16[2,256,1024]{1,2,0:T(8,128)(2,1)}, u32[]{:S(2)}, u32[]{:S(2)}) collective-permute-start(bf16[2,256,1024]{1,2,0:T(8,128)(2,1)S(1)} %collective-permute-done.1), channel_id=1, source_target_pairs={{0,8},{4,12},{1,9},{5,13},{2,10},{6,14},{3,11},{7,15},{16,24},{20,... | collective-permute-start | bytes 3145736 | tf_op jit(solution)/shard_map/ppermute | solution.py:15
  69.0 1.9 collective-permute-start.3
  71.1 42.2 %collective-permute-done.2 = bf16[2,256,1024]{1,2,0:T(8,128)(2,1)} collective-permute-done((bf16[2,256,1024]{1,2,0:T(8,128)(2,1)S(1)}, bf16[2,256,1024]{1,2,0:T(8,128)(2,1)}, u32[]{:S(2)}, u32[]{:S(2)}) %collective-permute-start.2) | collective-permute-done | bytes 1048608 | tf_op jit(solution)/shard_map/ppermute | solution.py:15
  113.3 22.5 %collective-permute-done.3 = bf16[2,256,1024]{1,2,0:T(8,128)(2,1)} collective-permute-done((bf16[2,256,1024]{1,2,0:T(8,128)(2,1)S(1)}, bf16[2,256,1024]{1,2,0:T(8,128)(2,1)}, u32[]{:S(2)}, u32[]{:S(2)}) %collective-permute-start.3) | collective-permute-done | bytes 1048608 | tf_op jit(solution)/shard_map/ppermute | solution.py:15
  135.7 2.9 pad_maximum_fusion.1
  138.7 20.0 %conditional.3 = (bf16[2,256,1024]{1,2,0:T(8,128)(2,1)}) conditional(s32[]{:T(128)} %convert_element_type.158, () %tuple.23, (bf16[2,256,1024]{1,2,0:T(8,128)(2,1)S(1)}, f32[1024]{0:T(1024)S(1)}, bf16[2,768,1024]{1,2,0:T(8,128)(2,1)}, f32[1024]{0:T(1024)S(1)}, s32[2,4]{1,0:T(2,128)S(1)}, /*index=5*/s32[]{:T(128)}) %tuple.62), branch_computations={%region_3.4_spmd, %region_4.11_spmd} | conditional | flops 825910528 | bytes 54910304 | solution.py:112
  139.7 2.5 multiply_convert_fusion
  142.3 1.3 multiply_convert_fusion.1
  143.6 15.1 %while.9 = (s32[]{:T(128)}, bf16[2,256,1024]{1,2,0:T(8,128)(2,1)}, bf16[2,768,8,128]{1,3,2,0:T(8,128)(2,1)}, pred[2,256,768]{2,1,0:T(8,128)(4,1)S(1)}, bf16[2,25...) while((s32[]{:T(128)}, bf16[2,256,1024]{1,2,0:T(8,128)(2,1)}, ...), condition=%wide.region_10.10_spmd, body=%wide.region_7.9_spmd.sunk | while | flops 818414336 | bytes 37308016 | solution.py:107
  143.6 2.1 fusion.56
  145.7 3.4 fusion.57
  149.1 1.1 fusion.58
  150.3 0.8 constant_dynamic-update-slice_fusion.2
  151.1 2.1 fusion.56
  153.2 3.4 fusion.57
  156.7 1.1 fusion.58
  157.8 0.8 constant_dynamic-update-slice_fusion.2
  158.7 2.3 copy.26
  161.7 35.2 %all-gather.3.cloned.1.call-done = bf16[2,256,4096]{2,1,0:T(8,128)(2,1)} async-done(((bf16[2,256,1024]{2,1,0:T(8,128)(2,1)}), bf16[2,256,4096]{2,1,0:T(8,128)(2,1)}) %all-gather.3.cloned.1.call-update) | async-done | bytes 4194320 | tf_op jit(solution)/shard_map/all_gather | solution.py:113
  196.9 285.2 %all-gather.5.cloned.1.call-done = bf16[4096,2048]{1,0:T(8,128)(2,1)} async-done(((bf16[1024,2048]{1,0:T(8,128)(2,1)}), bf16[4096,2048]{1,0:T(8,128)(2,1)}) %all-gather.5.cloned.1.call-update) | async-done | bytes 16777232 | tf_op jit(solution)/shard_map/all_gather | solution.py:117
  482.2 13.7 %convolution_convert_fusion = bf16[512,2048]{1,0:T(8,128)(2,1)S(1)} fusion(bf16[512,4096]{1,0:T(8,128)(2,1)} %bitcast.89, bf16[4096,2048]{1,0:T(8,128)(2,1)} %all-gather.5.cloned.1.call-done), kind=kOutput, calls=%fused_computation.61 | convolution fusion | flops 8590983168 | bytes 23068672 | tf_op jit(solution)/shard_map/dot_general | solution.py:115
  495.9 1.5 select_bitcast_fusion
  (38 shorter events, 2.5 us)
Async XLA Ops:
  6.5 190.4 %all-gather.3.cloned.1.call-start = ((), (), s32[]{:S(2)}) async-start(), calls=%async_computation | async-start | bytes 5242880 | tf_op jit(solution)/shard_map/all_gather | solution.py:113
  9.9 2.7 copy-start
  9.9 10.7 %copy-start.6 = (bf16[7,2048]{1,0:T(8,128)(2,1)S(1)}, bf16[7,2048]{1,0:T(8,128)(2,1)}, u32[]{:S(2)}) copy-start(bf16[7,2048]{1,0:T(8,128)(2,1)} %param.15) | copy-start | bytes 86020
  15.6 5.0 collective-permute-start
  20.8 117.8 %copy-start.1 = (bf16[2,256,2048]{2,1,0:T(8,128)(2,1)}, bf16[2,256,2048]{2,1,0:T(8,128)(2,1)S(1)}, u32[]{:S(2)}) copy-start(bf16[2,256,2048]{2,1,0:T(8,128)(2,1)S(1)} %get-tuple-element.182) | copy-start | bytes 6291460
  20.8 50.1 %copy-start.9 = (s32[2,4]{1,0:T(2,128)S(1)}, s32[2,4]{1,0:T(2,128)}, u32[]{:S(2)}) copy-start(s32[2,4]{1,0:T(2,128)} %param.19) | copy-start | bytes 100
  23.9 114.8 %copy-start.7 = (f32[1024]{0:T(1024)S(1)}, f32[1024]{0:T(1024)}, u32[]{:S(2)}) copy-start(f32[1024]{0:T(1024)} %param.16) | copy-start | bytes 12292
  23.9 114.8 %copy-start.8 = (f32[1024]{0:T(1024)S(1)}, f32[1024]{0:T(1024)}, u32[]{:S(2)}) copy-start(f32[1024]{0:T(1024)} %param.17) | copy-start | bytes 12292
  29.7 34.1 %collective-permute-start.1 = (bf16[2,256,1024]{1,2,0:T(8,128)(2,1)}, bf16[2,256,1024]{1,2,0:T(8,128)(2,1)S(1)}, u32[]{:S(2)}, u32[]{:S(2)}) collective-permute-start(bf16[2,256,1024]{1,2,0:T(8,128)(2,1)} %bitcast.81), channel_id=1, source_target_pairs={{0,16},{1,17},{2,18},{3,19},{4,20},{5,21},{6,22},{7,23},{8,24},{9,... | collective-permute-start | bytes 3145736 | tf_op jit(solution)/shard_map/ppermute | solution.py:15
  63.8 49.5 %collective-permute-start.2 = (bf16[2,256,1024]{1,2,0:T(8,128)(2,1)S(1)}, bf16[2,256,1024]{1,2,0:T(8,128)(2,1)}, u32[]{:S(2)}, u32[]{:S(2)}) collective-permute-start(bf16[2,256,1024]{1,2,0:T(8,128)(2,1)S(1)} %collective-permute-done.1), channel_id=1, source_target_pairs={{0,8},{4,12},{1,9},{5,13},{2,10},{6,14},{3,11},{7,15},{16,24},{20,... | collective-permute-start | bytes 3145736 | tf_op jit(solution)/shard_map/ppermute | solution.py:15
  69.0 66.8 %collective-permute-start.3 = (bf16[2,256,1024]{1,2,0:T(8,128)(2,1)S(1)}, bf16[2,256,1024]{1,2,0:T(8,128)(2,1)}, u32[]{:S(2)}, u32[]{:S(2)}) collective-permute-start(bf16[2,256,1024]{1,2,0:T(8,128)(2,1)S(1)} %collective-permute-done.1), channel_id=1, source_target_pairs={{0,4},{4,8},{8,12},{1,5},{5,9},{9,13},{2,6},{6,10},{10,14},{3,7},{... | collective-permute-start | bytes 3145736 | tf_op jit(solution)/shard_map/ppermute | solution.py:15
  138.7 1.0 copy-start.4
  139.7 2.6 copy-start.5
  145.7 3.4 copy-start.3
  153.2 3.4 copy-start.3
  161.0 321.2 %all-gather.5.cloned.1.call-start = ((), (), s32[]{:S(2)}) async-start(), calls=%async_computation.1 | async-start | bytes 20971520 | tf_op jit(solution)/shard_map/all_gather | solution.py:117
  482.2 13.8 %copy-start.2 = (bf16[2,256,2048]{2,1,0:T(8,128)(2,1)S(1)}, bf16[2,256,2048]{2,1,0:T(8,128)(2,1)}, u32[]{:S(2)}) copy-start(bf16[2,256,2048]{2,1,0:T(8,128)(2,1)} %copy-done.1) | copy-start | bytes 6291460
Sparse Core Ops, SparseCore 0:
  161.1 35.8 all-gather.2
  198.5 283.6 all-gather.4
where the time goes:
time: 509 us; the launch traced here: 504 us
  waiting for transfers between devices  420 us (83%)
  local copies, waits for them, and re-layouts  20.1 us (4%)
  matrix products  20.1 us (4%)
  other arithmetic  18.2 us (4%)
  between operations  13.5 us (3%)
  starting transfers between devices  11.8 us (2%)
    all_gather x1, waiting for transfers between devices, per_device(): lax.all_gather(out_weight, 'seq', axis=0, tiled=True)  285 us
    ppermute x4, waiting for transfers between devices, from_behind(): lax.ppermute(value, axis, [(source, source + steps) for source in range(f...  99.3 us
    all_gather x1, waiting for transfers between devices, per_device(): all_heads = lax.all_gather(mixed, 'tensor', axis=2, tiled=True)  35.2 us
    dot_general x1, matrix products, per_device(): jnp.dot(flattened, lax.all_gather(out_weight, 'seq', axis=0, tiled=True),...  13.7 us
    unnamed x16, local copies, waits for them, and re-layouts  11.8 us
    ppermute x4, starting transfers between devices, from_behind(): lax.ppermute(value, axis, [(source, source + steps) for source in range(f...  11.6 us
  transfers between devices with their start and end apart: 6, of which 6 were waited for; matrix products, arithmetic and copies ran while one was open for 0% of the time, Pallas kernels for 0%

commit v1 on v0

--- a/solution.py
+++ b/solution.py
@@ -1,9 +1,16 @@
+import functools
+
 import jax
 import jax.numpy as jnp
 from jax import lax
+from jax.experimental import pallas as pl
+from jax.experimental.pallas import tpu as pltpu
 from jax.sharding import PartitionSpec as P
 
 HD = 128
+MESH = pl.DeviceIdType.MESH
+HALO = 16
+PARTS = 4
 
 
 NEG_FILL = -1e30
@@ -19,7 +26,7 @@
     return jnp.sum((contig_ends[:, None, :] <= positions[None, :, None]).astype(jnp.int32), axis=2)
 
 
-def per_device(resid, streams, filt, q_gain, k_gain, out_weight, contig_lengths):
+def weights_travel(resid, streams, filt, q_gain, k_gain, out_weight, contig_lengths):
     resid_own = resid[0]
     streams_own = streams[0]
     tap_count = filt.shape[0]
@@ -122,7 +129,357 @@
     return output[None]
 
 
+def hyena_kernel(stream_ref, resid_ref, prev_ref, filt_ref, hidden_ref, attend_ref, extended):
+    taps, rows, width = filt_ref.shape[0], resid_ref.shape[1], resid_ref.shape[2]
+    gate, value = stream_ref[0, 0].astype(jnp.float32), stream_ref[0, 2].astype(jnp.float32)
+    extended[:HALO] = prev_ref[0].astype(jnp.float32)
+    extended[HALO:] = (gate * value).astype(jnp.bfloat16).astype(jnp.float32)
+    step = 64
+    for col in range(0, width, HD):
+        lanes = slice(col, col + HD)
+        tap_rows = [filt_ref[j : j + 1, lanes].astype(jnp.float32) for j in range(taps)]
+        for row in range(0, rows, step):
+            conv = jnp.zeros((step, HD), jnp.float32)
+            for j in range(taps):
+                begin = HALO + row - j
+                conv = conv + tap_rows[j] * extended[begin : begin + step, lanes]
+            own = slice(row, row + step)
+            out_gate = stream_ref[0, 1, own, lanes].astype(jnp.float32)
+            hidden = (resid_ref[0, own, lanes].astype(jnp.float32) + out_gate * conv).astype(jnp.bfloat16)
+            hidden_ref[0, own, lanes] = hidden
+            if col // HD % 2 == 0:
+                attend_ref[0, 0, own, col // 2 : col // 2 + HD] = hidden
+
+
+def run_hyena(streams, resid, prev, filt, pieces):
+    batch, _, rows, width = streams.shape
+    block = width // pieces
+    return pl.pallas_call(
+        hyena_kernel,
+        grid=(batch, pieces),
+        in_specs=[
+            pl.BlockSpec((1, 3, rows, block), lambda m, k: (m, 0, 0, k)),
+            pl.BlockSpec((1, rows, block), lambda m, k: (m, 0, k)),
+            pl.BlockSpec((1, HALO, block), lambda m, k: (m, 0, k)),
+            pl.BlockSpec((filt.shape[0], block), lambda m, k: (0, k)),
+        ],
+        out_specs=[
+            pl.BlockSpec((1, rows, block), lambda m, k: (m, 0, k)),
+            pl.BlockSpec((1, 1, rows, block // 2), lambda m, k: (m, k, 0, 0)),
+        ],
+        out_shape=[
+            jax.ShapeDtypeStruct((batch, rows, width), jnp.bfloat16),
+            jax.ShapeDtypeStruct((batch, pieces, rows, block // 2), jnp.bfloat16),
+        ],
+        scratch_shapes=[pltpu.VMEM((HALO + rows, block), jnp.float32)],
+        compiler_params=pltpu.CompilerParams(vmem_limit_bytes=32 << 20),
+        name="hyena",
+    )(streams, resid, prev, filt)
+
+
+def landed(ref, sem):
+    pltpu.make_async_copy(ref, ref, sem).wait()
+
+
+def attention_kernel(
+    n_seq, n_tensor, rows, attend_ref, gains_ref, begin_ref, weight_ref, out_ref,
+    tokens, gains, queries, keys, own_mixed, mixed, weight, partial,
+    send_a, recv_a, send_b, recv_b, send_y, recv_y,
+    tok_send, tok_recv, gain_send, gain_recv, weight_sem, mix_send, mix_recv, mix_local,
+    a_send, a_recv, b_send, b_recv, y_send, y_recv,
+):
+    pipe, seq, tensor = (lax.axis_index(name) for name in ("pipe", "seq", "tensor"))
+    piece = tokens.shape[1]
+    half = seq // 2
+    inner = seq + half * (3 - 2 * seq)
+    me = (pipe * n_seq + seq) * n_tensor + tensor
+    world = 2 * n_seq * n_tensor
+    barrier = pltpu.get_barrier_semaphore()
+
+    fetch = pltpu.make_async_copy(weight_ref, weight, weight_sem)
+    fetch.start()
+
+    def greet(step, carry):
+        other = lax.rem(me + step, world)
+        device = (other // (n_seq * n_tensor), other // n_tensor % n_seq, other % n_tensor)
+        pl.semaphore_signal(barrier, inc=1, device_id=device, device_id_type=MESH)
+        return carry
+
+    lax.fori_loop(1, world, greet, 0)
+    pl.semaphore_wait(barrier, world - 1)
+
+    def remote(source, target, send_sem, recv_sem, device):
+        return pltpu.make_async_remote_copy(
+            src_ref=source, dst_ref=target, send_sem=send_sem, recv_sem=recv_sem,
+            device_id=device, device_id_type=MESH,
+        )
+
+    def deliver(wait):
+        for batch in range(2):
+            for other in range(n_tensor):
+                slot = batch * n_tensor + other
+                is_self = (seq == tensor) & (other == tensor) if batch == 0 else None
+                source = attend_ref.at[batch, other]
+                target = tokens.at[pl.ds(pl.multiple_of(seq * rows, rows), rows)]
+                far = remote(source, target, tok_send.at[slot], tok_recv.at[seq], (batch, tensor, other))
+                gain_far = remote(gains_ref.at[other], gains, gain_send.at[slot], gain_recv.at[0], (batch, tensor, other))
+                away = True if is_self is None else jnp.logical_not(is_self)
+
+                @pl.when(away)
+                def _():
+                    far.wait_send() if wait else far.start()
+
+                @pl.when(away & (seq == 0))
+                def _():
+                    gain_far.wait_send() if wait else gain_far.start()
+
+                if is_self is not None and not wait:
+
+                    @pl.when(is_self)
+                    def _():
+                        pltpu.make_async_copy(source, target, tok_recv.at[seq]).start()
+
+                    @pl.when(is_self & (seq == 0))
+                    def _():
+                        pltpu.make_async_copy(gains_ref.at[other], gains, gain_recv.at[0]).start()
+
+    @pl.when(pipe == 0)
+    def _():
+        deliver(False)
+
+    landed(gains, gain_recv.at[0])
+    for source in range(n_seq):
+        here = slice(source * rows, (source + 1) * rows)
+        landed(tokens.at[here], tok_recv.at[source])
+        block = tokens[here].astype(jnp.float32)
+        queries[here] = (block * gains[0:1]).astype(jnp.bfloat16)
+        keys[here] = (block * gains[1:2]).astype(jnp.bfloat16)
+
+    window = min(3, n_seq) * rows
+    mine = pl.ds(pl.multiple_of(tensor * piece, piece), piece)
+
+    def chunk_of(step):
+        order = (3 - step) + (step // 2) * (inner * (2 * step - 5))
+        return order + half * (3 - 2 * order)
+
+    def mix_copy(step, hop):
+        return remote(
+            own_mixed.at[step], mixed.at[step, :, mine], mix_send.at[step, hop - 1],
+            mix_recv.at[step, tensor], (pipe, seq, lax.rem(tensor + hop, n_tensor)),
+        )
+
+    def attention(step):
+        chunk = chunk_of(step)
+        first = pl.multiple_of(chunk * rows, rows)
+        low = pl.multiple_of((chunk // 3) * rows, rows)
+        position = first + lax.broadcasted_iota(jnp.int32, (rows, window), 0)
+        key_position = low + lax.broadcasted_iota(jnp.int32, (rows, window), 1)
+        visible = (key_position >= begin_ref[pl.ds(first, rows)]) & (key_position <= position)
+        for head in range(piece // HD):
+            lanes = slice(head * HD, (head + 1) * HD)
+            scores = lax.dot_general(
+                queries[pl.ds(first, rows), lanes], keys[pl.ds(low, window), lanes],
+                (((1,), (1,)), ((), ())), preferred_element_type=jnp.float32,
+            ) * (1.0 / HD)
+            scores = jnp.where(visible, scores, NEG_FILL)
+            weights = jnp.exp(scores - jnp.max(scores, axis=1, keepdims=True))
+            total = jnp.sum(weights, axis=1, keepdims=True)
+            result = jnp.dot(
+                weights.astype(jnp.bfloat16), tokens[pl.ds(low, window), lanes],
+                preferred_element_type=jnp.float32,
+            )
+            own_mixed[step, :, lanes] = (result / total).astype(jnp.bfloat16)
+        pltpu.make_async_copy(own_mixed.at[step], mixed.at[step, :, mine], mix_local.at[step]).start()
+        for hop in range(1, n_tensor):
+            mix_copy(step, hop).start()
+
+    def inward(step, part):
+        return remote(
+            send_a.at[step, part], recv_a.at[step, part], a_send.at[step, part],
+            a_recv.at[step, part], (pipe, 1 + half, tensor),
+        )
+
+    def project(step):
+        pltpu.make_async_copy(own_mixed.at[step], mixed.at[step, :, mine], mix_local.at[step]).wait()
+        for hop in range(1, n_tensor):
+            source = lax.rem(tensor + hop, n_tensor)
+            lanes = pl.ds(pl.multiple_of(source * piece, piece), piece)
+            landed(mixed.at[step, :, lanes], mix_recv.at[step, source])
+        width = partial.shape[3]
+        for part in range(PARTS):
+            value = jnp.dot(
+                mixed[step], weight[:, part * width : (part + 1) * width],
+                preferred_element_type=jnp.float32,
+            )
+            partial[step, part] = value
+
+            @pl.when((inner == 0) & (step < 3))
+            def _():
+                send_a[step, part] = value.astype(jnp.bfloat16)
+                inward(step, part).start()
+
+    def turn(step, carry):
+        @pl.when(step < 4)
+        def _():
+            attention(step)
+
+        @pl.when(step == 1)
+        def _():
+            fetch.wait()
+
+        @pl.when(step > 0)
+        def _():
+            project(step - 1)
+
+        return carry
+
+    lax.fori_loop(0, 5, turn, 0)
+
+    def across(step, part):
+        return remote(
+            send_a.at[step, part], recv_b.at[step, part], b_send.at[step, part],
+            b_recv.at[step, part], (pipe, 3 - seq, tensor),
+        )
+
+    def outward(part):
+        return remote(
+            send_b.at[part], recv_b.at[0, part], b_send.at[2, part],
+            b_recv.at[0, part], (pipe, 3 * half, tensor),
+        )
+
+    def home(part):
+        return remote(
+            send_y.at[part], recv_y.at[part], y_send.at[part], y_recv.at[part], (1, seq, tensor)
+        )
+
+    def finish(part, value):
+        width = value.shape[1]
+
+        @pl.when(pipe == 0)
+        def _():
+            send_y[part] = value.astype(jnp.bfloat16)
+            home(part).start()
+
+        @pl.when(pipe == 1)
+        def _():
+            out_ref[1, :, part * width : (part + 1) * width] = value.astype(jnp.bfloat16)
+
+    def forward(step, part):
+        landed(recv_a.at[step, part], a_recv.at[step, part])
+        send_a[step, part] = (partial[step, part] + recv_a[step, part].astype(jnp.float32)).astype(jnp.bfloat16)
+        across(step, part).start()
+
+    def relay(part):
+        landed(recv_b.at[0, part], b_recv.at[0, part])
+        send_b[part] = (partial[2, part] + recv_b[0, part].astype(jnp.float32)).astype(jnp.bfloat16)
+        outward(part).start()
+
+    @pl.when(inner == 1)
+    def _():
+        for part in range(PARTS):
+            forward(0, part)
+            if part > 0:
+                relay(part - 1)
+        relay(PARTS - 1)
+        for part in range(PARTS):
+            forward(1, part)
+        for part in range(PARTS):
+            landed(recv_a.at[2, part], a_recv.at[2, part])
+            landed(recv_b.at[1, part], b_recv.at[1, part])
+            finish(part, partial[3, part] + recv_a[2, part].astype(jnp.float32) + recv_b[1, part].astype(jnp.float32))
+        for part in range(PARTS):
+            across(0, part).wait_send()
+            across(1, part).wait_send()
+            outward(part).wait_send()
+
+    @pl.when(inner == 0)
+    def _():
+        for part in range(PARTS):
+            landed(recv_b.at[0, part], b_recv.at[0, part])
+            finish(part, partial[3, part] + recv_b[0, part].astype(jnp.float32))
+        for step in range(3):
+            for part in range(PARTS):
+                inward(step, part).wait_send()
+
+    @pl.when(pipe == 1)
+    def _():
+        width = recv_y.shape[2]
+        for part in range(PARTS):
+            landed(recv_y.at[part], y_recv.at[part])
+            out_ref[0, :, part * width : (part + 1) * width] = recv_y[part]
+
+    @pl.when(pipe == 0)
+    def _():
+        for part in range(PARTS):
+            home(part).wait_send()
+        deliver(True)
+
+    for step in range(4):
+        for hop in range(1, n_tensor):
+            mix_copy(step, hop).wait_send()
+
+
+def run_attention(attend, gains, begins, weight, n_seq, n_tensor):
+    batch, pieces, rows, piece = attend.shape
+    depth, width = weight.shape
+    length = n_seq * rows
+    part = width // PARTS
+    bf16, f32 = jnp.bfloat16, jnp.float32
+    dma = pltpu.SemaphoreType.DMA
+    anywhere, vmem = pl.BlockSpec(memory_space=pl.ANY), pl.BlockSpec(memory_space=pltpu.VMEM)
+    return pl.pallas_call(
+        functools.partial(attention_kernel, n_seq, n_tensor, rows),
+        in_specs=[anywhere, anywhere, vmem, anywhere],
+        out_specs=vmem,
+        out_shape=jax.ShapeDtypeStruct((batch, rows, width), bf16),
+        scratch_shapes=[
+            pltpu.VMEM((length, piece), bf16),
+            pltpu.VMEM(gains.shape[1:], f32),
+            pltpu.VMEM((length, piece), bf16),
+            pltpu.VMEM((length, piece), bf16),
+            pltpu.VMEM((4, rows, piece), bf16),
+            pltpu.VMEM((4, rows, depth), bf16),
+            pltpu.VMEM((depth, width), bf16),
+            pltpu.VMEM((4, PARTS, rows, part), f32),
+            pltpu.VMEM((3, PARTS, rows, part), bf16),
+            pltpu.VMEM((3, PARTS, rows, part), bf16),
+            pltpu.VMEM((PARTS, rows, part), bf16),
+            pltpu.VMEM((2, PARTS, rows, part), bf16),
+            pltpu.VMEM((PARTS, rows, part), bf16),
+            pltpu.VMEM((PARTS, rows, part), bf16),
+            dma((2 * n_tensor,)), dma((n_seq,)), dma((2 * n_tensor,)), dma((1,)), dma,
+            dma((4, n_tensor - 1)), dma((4, n_tensor)), dma((4,)),
+            dma((3, PARTS)), dma((3, PARTS)), dma((3, PARTS)), dma((2, PARTS)),
+            dma((PARTS,)), dma((PARTS,)),
+        ],
+        compiler_params=pltpu.CompilerParams(
+            collective_id=0, has_side_effects=True, vmem_limit_bytes=56 << 20
+        ),
+        name="attention_projection",
+    )(attend, gains, begins, weight)
+
+
+def sums_travel(resid, streams, filt, q_gain, k_gain, out_weight, contig_lengths):
+    n_seq, n_tensor = lax.axis_size("seq"), lax.axis_size("tensor")
+    section = lax.axis_index("pipe")
+    batch, rows = resid.shape[1:3]
+    tail = streams[0, :, rows - HALO :].astype(jnp.float32)
+    prev = from_behind((tail[:, :, 0] * tail[:, :, 2]).astype(jnp.bfloat16), "seq", 1)
+    hidden, attend = run_hyena(
+        jnp.transpose(streams[0], (0, 2, 1, 3)), resid[0], prev, filt, n_tensor
+    )
+    gains = jnp.stack([q_gain.reshape(n_tensor, -1), k_gain.reshape(n_tensor, -1)], axis=1)
+    gains = jnp.pad(gains, ((0, 0), (0, 6), (0, 0)))
+    ends = jnp.cumsum(jnp.where(section == 0, contig_lengths[0], contig_lengths[1]))
+    position = jnp.arange(n_seq * rows, dtype=jnp.int32)
+    begins = jnp.max(jnp.where(ends[None] <= position[:, None], ends[None], 0), axis=1, keepdims=True)
+    projected = run_attention(attend, gains, begins.astype(jnp.int32), out_weight, n_seq, n_tensor)
+    return jnp.where(section == 0, hidden, projected)[None]
+
+
 def solution(mesh):
+    few = mesh.shape["seq"] == 4 and mesh.shape["tensor"] == 4 and mesh.shape["pipe"] == 2
+    per_device = sums_travel if few else weights_travel
     placed = (
         P("pipe", None, "seq", "tensor"),
         P("pipe", None, "seq", None, "tensor"),

time: 509 us -> 154 us (0.30)
  waiting for transfers between devices: 420 us -> 0.36 us
  Pallas kernels: 0 us -> 139 us
  matrix products: 20.1 us -> 0 us
  local copies, waits for them, and re-layouts: 20.1 us -> 4.79 us
  between operations: 13.5 us -> 0.08 us
  other arithmetic: 18.2 us -> 6.02 us
  starting transfers between devices: 11.8 us -> 3.2 us
    all_gather x2 -> x0, waiting for transfers between devices: 320 us -> none  [the longest x1 285 us: per_device(): lax.all_gather(out_weight, 'seq', axis=0, tiled=True)]
    pallas_call x0 -> x2, Pallas kernels: none -> 139 us  [the longest x1 133 us: run_attention(): pl.pallas_call(functools.partial(attention_kernel, n_seq, n_tensor, rows)...]
    ppermute x4 -> x1, waiting for transfers between devices: 99.3 us -> 0.36 us  [from_behind(): lax.ppermute(value, axis, [(source, source + steps) for source in range(f...]
    dot_general x5 -> x0, matrix products: 20.1 us -> none  [the longest x1 13.7 us: per_device(): jnp.dot(flattened, lax.all_gather(out_weight, 'seq', axis=0, tiled=True),...]
    ppermute x4 -> x1, starting transfers between devices: 11.6 us -> 3.2 us  [from_behind(): lax.ppermute(value, axis, [(source, source + steps) for source in range(f...]
    unnamed x16 -> x12, local copies, waits for them, and re-layouts: 11.8 us -> 3.77 us
    sub x2 -> x0, other arithmetic: 6.85 us -> none  [one_batch(): weights = jnp.where(visible_part[None], jnp.exp(scores - top), 0.0)]
  transfers between devices with their start and end apart: 6 -> 1, of which waited for: 6 -> 1; matrix products, arithmetic and copies ran while one was open for 0% -> 2% of each run, Pallas kernels for 0% -> 0%
where the time goes in v1:
time: 154 us
  Pallas kernels  139 us (90%)
  other arithmetic  6.02 us (4%)
  local copies, waits for them, and re-layouts  4.79 us (3%)
  starting transfers between devices  3.2 us (2%)
    pallas_call x1, Pallas kernels, run_attention(): pl.pallas_call(functools.partial(attention_kernel, n_seq, n_tensor, rows)...  133 us
    pallas_call x1, Pallas kernels, run_hyena(): pl.pallas_call(hyena_kernel, grid=(batch, pieces), in_specs=[pl.BlockSpec...  6.39 us
    unnamed x12, local copies, waits for them, and re-layouts  3.77 us
    ppermute x1, starting transfers between devices, from_behind(): lax.ppermute(value, axis, [(source, source + steps) for source in range(f...  3.2 us
    broadcast_in_dim x1, other arithmetic, sums_travel(): return jnp.where(section == 0, hidden, projected)[None]  3.14 us
  transfers between devices with their start and end apart: 1, of which 1 were waited for; matrix products, arithmetic and copies ran while one was open for 2% of the time, Pallas kernels for 0%

profile of v1, /device:TPU:13, one launch (start us, length us, event | category | flops | bytes accessed | tf_op | source)
XLA Modules:
  0.0 153.8 jit_solution(10832431777613332045)
XLA Ops:
  0.0 0.0 copy-start.4
  0.0 0.0 copy-start.5
  0.0 0.0 copy-start.3
  0.0 0.0 copy-start.1
  0.0 1.2 fusion
  1.3 3.2 %collective-permute-start = (bf16[2,16,2048]{2,1,0:T(8,128)(2,1)S(1)}, bf16[2,16,2048]{2,1,0:T(8,128)(2,1)S(1)}, u32[]{:S(2)}, u32[]{:S(2)}) collective-permute-start(bf16[2,16,2048]{2,1,0:T(8,128)(2,1)S(1)} %fusion.2), channel_id=1, source_target_pairs={{0,4},{4,8},{8,12},{1,5},{5,9},{9,13},{2,6},{6,10},{10,14},{3,7},{... | collective-permute-start | bytes 393224 | tf_op jit(solution)/shard_map/ppermute | solution.py:22
  4.5 0.8 fusion.3
  5.3 0.2 reduce-window.8
  5.4 0.1 select_reduce_fusion
  5.5 1.0 copy.12.begin_ref
  6.5 0.0 copy-done.4
  6.6 0.0 copy-done.5
  6.6 0.6 select_maximum_fusion.gains_ref
  7.2 0.4 collective-permute-done.prev_ref
  7.5 0.0 copy-done.3
  7.5 0.0 copy-done.1
  7.5 0.0 copy-start
  7.5 2.8 %copy-done = bf16[1,2,256,3,2048]{4,2,3,1,0:T(8,128)(2,1)S(1)} copy-done((bf16[1,2,256,3,2048]{4,2,3,1,0:T(8,128)(2,1)S(1)}, bf16[1,2,256,3,2048]{4,2,3,1,0:T(8,128)(2,1)}, u32[]{:S(2)}) %copy-start) | copy-done | bytes 6291480
  10.3 6.4 %hyena.1 = (bf16[2,256,2048]{2,1,0:T(8,128)(2,1)S(1)}, bf16[2,4,256,256]{3,2,1,0:T(8,128)(2,1)S(1)}) custom-call(bf16[2,3,256,2048]{3,2,1,0:T(8,128)(2,1)S(1)} %bitcast.19, bf16[2,256,2048]{2,1,0:T(8,128)(2,1)S(1)} %bitcast.20, bf16[2,16,2048]{2,1,0:T(8,128)(2,1)S(1)} %collective-permute-done.prev_ref, bf16[7,2048]{1,0:T(8,128)(2,1)S(1)} %copy-done.3), custom_call_target="tpu_custom_call" | custom-call | tf_op jit(solution)/shard_map/hyena/pallas_call | solution.py:157
  16.7 0.0 copy-start.2
  16.7 1.0 copy-done.2
  17.7 132.9 %attention_projection.1 = bf16[2,256,2048]{2,1,0:T(8,128)(2,1)} custom-call(bf16[2,4,256,256]{3,2,1,0:T(8,128)(2,1)} %copy-done.2, f32[4,8,256]{2,1,0:T(8,128)} %select_maximum_fusion.gains_ref, s32[1024,1]{1,0:T(8,128)} %copy.12.begin_ref, bf16[1024,2048]{1,0:T(8,128)(2,1)} %weight_ref.1), custom_call_target="tpu_custom_call" | custom-call | tf_op jit(solution)/shard_map/attention_projection/pallas_call | solution.py:430
  150.6 3.1 %select_bitcast_fusion = bf16[1,2,256,2048]{3,2,1,0:T(8,128)(2,1)} fusion(bf16[2,256,2048]{2,1,0:T(8,128)(2,1)S(1)} %get-tuple-element.7, bf16[2,256,2048]{2,1,0:T(8,128)(2,1)} %attention_projection.1, pred[]{:T(512)S(6)} %eq.4), kind=kLoop, calls=%fused_computation | loop fusion | flops 1048576 | bytes 6291457 | tf_op jit(solution)/shard_map/broadcast_in_dim | solution.py:477
  (1 shorter events, 0.0 us)
Async XLA Ops:
  0.0 6.5 %copy-start.4 = (f32[1024]{0:T(1024)S(1)}, f32[1024]{0:T(1024)}, u32[]{:S(2)}) copy-start(f32[1024]{0:T(1024)} %param.11) | copy-start | bytes 12292
  0.0 6.6 %copy-start.5 = (f32[1024]{0:T(1024)S(1)}, f32[1024]{0:T(1024)}, u32[]{:S(2)}) copy-start(f32[1024]{0:T(1024)} %param.10) | copy-start | bytes 12292
  0.0 7.5 %copy-start.3 = (bf16[7,2048]{1,0:T(8,128)(2,1)S(1)}, bf16[7,2048]{1,0:T(8,128)(2,1)}, u32[]{:S(2)}) copy-start(bf16[7,2048]{1,0:T(8,128)(2,1)} %filt_ref.1) | copy-start | bytes 86020
  0.0 7.5 %copy-start.1 = (bf16[1,2,256,2048]{3,2,1,0:T(8,128)(2,1)S(1)}, bf16[1,2,256,2048]{3,2,1,0:T(8,128)(2,1)}, u32[]{:S(2)}) copy-start(bf16[1,2,256,2048]{3,2,1,0:T(8,128)(2,1)} %param.7) | copy-start | bytes 6291460
  1.3 6.3 %collective-permute-start = (bf16[2,16,2048]{2,1,0:T(8,128)(2,1)S(1)}, bf16[2,16,2048]{2,1,0:T(8,128)(2,1)S(1)}, u32[]{:S(2)}, u32[]{:S(2)}) collective-permute-start(bf16[2,16,2048]{2,1,0:T(8,128)(2,1)S(1)} %fusion.2), channel_id=1, source_target_pairs={{0,4},{4,8},{8,12},{1,5},{5,9},{9,13},{2,6},{6,10},{10,14},{3,7},{... | collective-permute-start | bytes 393224 | tf_op jit(solution)/shard_map/ppermute | solution.py:22
  7.5 2.8 %copy-start = (bf16[1,2,256,3,2048]{4,2,3,1,0:T(8,128)(2,1)S(1)}, bf16[1,2,256,3,2048]{4,2,3,1,0:T(8,128)(2,1)}, u32[]{:S(2)}) copy-start(bf16[1,2,256,3,2048]{4,2,3,1,0:T(8,128)(2,1)} %param.8) | copy-start | bytes 18874372
  16.7 1.0 copy-start.2

commit v2 on v1

--- a/solution.py
+++ b/solution.py
@@ -10,7 +10,7 @@
 HD = 128
 MESH = pl.DeviceIdType.MESH
 HALO = 16
-PARTS = 4
+PARTS = 8
 
 
 NEG_FILL = -1e30
@@ -129,62 +129,16 @@
     return output[None]
 
 
-def hyena_kernel(stream_ref, resid_ref, prev_ref, filt_ref, hidden_ref, attend_ref, extended):
-    taps, rows, width = filt_ref.shape[0], resid_ref.shape[1], resid_ref.shape[2]
-    gate, value = stream_ref[0, 0].astype(jnp.float32), stream_ref[0, 2].astype(jnp.float32)
-    extended[:HALO] = prev_ref[0].astype(jnp.float32)
-    extended[HALO:] = (gate * value).astype(jnp.bfloat16).astype(jnp.float32)
-    step = 64
-    for col in range(0, width, HD):
-        lanes = slice(col, col + HD)
-        tap_rows = [filt_ref[j : j + 1, lanes].astype(jnp.float32) for j in range(taps)]
-        for row in range(0, rows, step):
-            conv = jnp.zeros((step, HD), jnp.float32)
-            for j in range(taps):
-                begin = HALO + row - j
-                conv = conv + tap_rows[j] * extended[begin : begin + step, lanes]
-            own = slice(row, row + step)
-            out_gate = stream_ref[0, 1, own, lanes].astype(jnp.float32)
-            hidden = (resid_ref[0, own, lanes].astype(jnp.float32) + out_gate * conv).astype(jnp.bfloat16)
-            hidden_ref[0, own, lanes] = hidden
-            if col // HD % 2 == 0:
-                attend_ref[0, 0, own, col // 2 : col // 2 + HD] = hidden
-
-
-def run_hyena(streams, resid, prev, filt, pieces):
-    batch, _, rows, width = streams.shape
-    block = width // pieces
-    return pl.pallas_call(
-        hyena_kernel,
-        grid=(batch, pieces),
-        in_specs=[
-            pl.BlockSpec((1, 3, rows, block), lambda m, k: (m, 0, 0, k)),
-            pl.BlockSpec((1, rows, block), lambda m, k: (m, 0, k)),
-            pl.BlockSpec((1, HALO, block), lambda m, k: (m, 0, k)),
-            pl.BlockSpec((filt.shape[0], block), lambda m, k: (0, k)),
-        ],
-        out_specs=[
-            pl.BlockSpec((1, rows, block), lambda m, k: (m, 0, k)),
-            pl.BlockSpec((1, 1, rows, block // 2), lambda m, k: (m, k, 0, 0)),
-        ],
-        out_shape=[
-            jax.ShapeDtypeStruct((batch, rows, width), jnp.bfloat16),
-            jax.ShapeDtypeStruct((batch, pieces, rows, block // 2), jnp.bfloat16),
-        ],
-        scratch_shapes=[pltpu.VMEM((HALO + rows, block), jnp.float32)],
-        compiler_params=pltpu.CompilerParams(vmem_limit_bytes=32 << 20),
-        name="hyena",
-    )(streams, resid, prev, filt)
-
-
 def landed(ref, sem):
     pltpu.make_async_copy(ref, ref, sem).wait()
 
 
 def attention_kernel(
-    n_seq, n_tensor, rows, attend_ref, gains_ref, begin_ref, weight_ref, out_ref,
+    n_seq, n_tensor, rows, streams_ref, resid_ref, filt_ref, gains_ref, begin_ref, weight_ref, out_ref,
+    streams, resid, tail, tail_gated, prev, extended, attend,
     tokens, gains, queries, keys, own_mixed, mixed, weight, partial,
     send_a, recv_a, send_b, recv_b, send_y, recv_y,
+    stream_sem, resid_sem, tail_sem, prev_send, prev_recv,
     tok_send, tok_recv, gain_send, gain_recv, weight_sem, mix_send, mix_recv, mix_local,
     a_send, a_recv, b_send, b_recv, y_send, y_recv,
 ):
@@ -197,6 +151,21 @@
     barrier = pltpu.get_barrier_semaphore()
 
     fetch = pltpu.make_async_copy(weight_ref, weight, weight_sem)
+    fetch_tail = pltpu.make_async_copy(streams_ref.at[:, :, pl.ds(rows - HALO, HALO)], tail, tail_sem)
+
+    def fetch_stream(batch):
+        return pltpu.make_async_copy(streams_ref.at[batch], streams.at[batch], stream_sem.at[batch])
+
+    def fetch_resid(batch):
+        return pltpu.make_async_copy(resid_ref.at[batch], resid.at[batch], resid_sem.at[batch])
+
+    @pl.when(pipe == 0)
+    def _():
+        fetch_tail.start()
+        for batch in (1, 0):
+            fetch_stream(batch).start()
+            fetch_resid(batch).start()
+
     fetch.start()
 
     def greet(step, carry):
@@ -214,38 +183,119 @@
             device_id=device, device_id_type=MESH,
         )
 
-    def deliver(wait):
-        for batch in range(2):
-            for other in range(n_tensor):
-                slot = batch * n_tensor + other
-                is_self = (seq == tensor) & (other == tensor) if batch == 0 else None
-                source = attend_ref.at[batch, other]
-                target = tokens.at[pl.ds(pl.multiple_of(seq * rows, rows), rows)]
-                far = remote(source, target, tok_send.at[slot], tok_recv.at[seq], (batch, tensor, other))
-                gain_far = remote(gains_ref.at[other], gains, gain_send.at[slot], gain_recv.at[0], (batch, tensor, other))
-                away = True if is_self is None else jnp.logical_not(is_self)
-
-                @pl.when(away)
-                def _():
-                    far.wait_send() if wait else far.start()
-
-                @pl.when(away & (seq == 0))
-                def _():
-                    gain_far.wait_send() if wait else gain_far.start()
-
-                if is_self is not None and not wait:
-
-                    @pl.when(is_self)
-                    def _():
-                        pltpu.make_async_copy(source, target, tok_recv.at[seq]).start()
-
-                    @pl.when(is_self & (seq == 0))
-                    def _():
-                        pltpu.make_async_copy(gains_ref.at[other], gains, gain_recv.at[0]).start()
+    def to_head_rows(turn):
+        batch, other = 1 - turn // n_tensor, turn % n_tensor
+        here = tokens.at[pl.ds(pl.multiple_of(seq * rows, rows), rows)]
+        device = (batch, tensor, other)
+        is_self = (batch == 0) & (seq == tensor) & (other == tensor)
+        return is_self, other, (
+            attend.at[batch, other], here, tok_send.at[turn], tok_recv.at[seq], device
+        ), (gains_ref.at[other], gains, gain_send.at[turn], gain_recv.at[0], device)
+
+    def send_turn(turn):
+        is_self, other, block, gain = to_head_rows(turn)
+
+        @pl.when(jnp.logical_not(is_self))
+        def _():
+            remote(*block).start()
+
+        @pl.when(jnp.logical_not(is_self) & (seq == 0))
+        def _():
+            remote(*gain).start()
+
+        @pl.when(is_self)
+        def _():
+            pltpu.make_async_copy(block[0], block[1], block[3]).start()
+
+        @pl.when(is_self & (seq == 0))
+        def _():
+            pltpu.make_async_copy(gain[0], gain[1], gain[3]).start()
+
+    def wait_turn(turn, carry):
+        is_self, other, block, gain = to_head_rows(turn)
+
+        @pl.when(jnp.logical_not(is_self))
+        def _():
+            remote(*block).wait_send()
+
+        @pl.when(jnp.logical_not(is_self) & (seq == 0))
+        def _():
+            remote(*gain).wait_send()
+
+        return carry
+
+    def send_prev():
+        return remote(tail_gated, prev, prev_send, prev_recv, (0, seq + 1, tensor))
+
+    def hyena(batch, column, keep):
+        lanes = pl.ds(pl.multiple_of(column, HD), HD)
+        taps = [filt_ref[j : j + 1, lanes].astype(jnp.float32) for j in range(filt_ref.shape[0])]
+        step = 64
+        for row in range(0, rows, step):
+            conv = jnp.zeros((step, HD), jnp.float32)
+            for j, tap in enumerate(taps):
+                conv = conv + tap * extended[batch, pl.ds(HALO + row - j, step), lanes]
+            own = pl.ds(row, step)
+            out_gate = streams[batch, 1, own, lanes].astype(jnp.float32)
+            hidden = resid[batch, own, lanes].astype(jnp.float32) + out_gate * conv
+            hidden = hidden.astype(jnp.bfloat16)
+            out_ref[batch, own, lanes] = hidden
+            keep(own, hidden)
 
     @pl.when(pipe == 0)
     def _():
-        deliver(False)
+        fetch_tail.wait()
+        tail_gated[...] = (
+            tail[:, 0].astype(jnp.float32) * tail[:, 2].astype(jnp.float32)
+        ).astype(jnp.bfloat16)
+
+        @pl.when(seq < n_seq - 1)
+        def _():
+            send_prev().start()
+
+        for batch in (1, 0):
+            fetch_stream(batch).wait()
+
+            def gate(strip, carry):
+                own = pl.ds(pl.multiple_of(strip * 16, 16), 16)
+                here = pl.ds(pl.multiple_of(HALO + strip * 16, 16), 16)
+                gated = streams[batch, 0, own].astype(jnp.float32) * streams[batch, 2, own].astype(jnp.float32)
+                extended[batch, here] = gated.astype(jnp.bfloat16).astype(jnp.float32)
+                return carry
+
+            lax.fori_loop(0, rows // 16, gate, 0)
+
+        @pl.when(seq == 0)
+        def _():
+            extended[:, :HALO] = jnp.zeros((2, HALO, extended.shape[2]), jnp.float32)
+
+        @pl.when(seq > 0)
+        def _():
+            landed(prev, prev_recv)
+            extended[:, :HALO] = prev[...].astype(jnp.float32)
+
+        for batch in (1, 0):
+            fetch_resid(batch).wait()
+
+        def attended(turn, carry):
+            batch, other = 1 - turn // n_tensor, turn % n_tensor
+            for head in range(piece // HD):
+
+                def keep(own, hidden):
+                    attend[batch, other, own, head * HD : (head + 1) * HD] = hidden
+
+                hyena(batch, (other * (piece // HD) + head) * 2 * HD, keep)
+            send_turn(turn)
+            return carry
+
+        def unattended(turn, carry):
+            batch, other = 1 - turn // n_tensor, turn % n_tensor
+            for head in range(piece // HD):
+                hyena(batch, (other * (piece // HD) + head) * 2 * HD + HD, lambda own, hidden: None)
+            return carry
+
+        lax.fori_loop(0, 2 * n_tensor, attended, 0)
+        lax.fori_loop(0, 2 * n_tensor, unattended, 0)
 
     landed(gains, gain_recv.at[0])
     for source in range(n_seq):
@@ -412,15 +462,20 @@
     def _():
         for part in range(PARTS):
             home(part).wait_send()
-        deliver(True)
+        lax.fori_loop(0, 2 * n_tensor, wait_turn, 0)
+
+        @pl.when(seq < n_seq - 1)
+        def _():
+            send_prev().wait_send()
 
     for step in range(4):
         for hop in range(1, n_tensor):
             mix_copy(step, hop).wait_send()
 
 
-def run_attention(attend, gains, begins, weight, n_seq, n_tensor):
-    batch, pieces, rows, piece = attend.shape
+def run_sections(streams, resid, filt, gains, begins, weight, n_seq, n_tensor):
+    batch, rows = resid.shape[:2]
+    piece = gains.shape[2]
     depth, width = weight.shape
     length = n_seq * rows
     part = width // PARTS
@@ -429,10 +484,17 @@
     anywhere, vmem = pl.BlockSpec(memory_space=pl.ANY), pl.BlockSpec(memory_space=pltpu.VMEM)
     return pl.pallas_call(
         functools.partial(attention_kernel, n_seq, n_tensor, rows),
-        in_specs=[anywhere, anywhere, vmem, anywhere],
+        in_specs=[anywhere, anywhere, vmem, anywhere, vmem, anywhere],
         out_specs=vmem,
         out_shape=jax.ShapeDtypeStruct((batch, rows, width), bf16),
         scratch_shapes=[
+            pltpu.VMEM(streams.shape, bf16),
+            pltpu.VMEM(resid.shape, bf16),
+            pltpu.VMEM((batch, 3, HALO, width), bf16),
+            pltpu.VMEM((batch, HALO, width), bf16),
+            pltpu.VMEM((batch, HALO, width), bf16),
+            pltpu.VMEM((batch, HALO + rows, width), f32),
+            pltpu.VMEM((batch, n_tensor, rows, piece), bf16),
             pltpu.VMEM((length, piece), bf16),
             pltpu.VMEM(gains.shape[1:], f32),
             pltpu.VMEM((length, piece), bf16),
@@ -447,6 +509,7 @@
             pltpu.VMEM((2, PARTS, rows, part), bf16),
             pltpu.VMEM((PARTS, rows, part), bf16),
             pltpu.VMEM((PARTS, rows, part), bf16),
+            dma((batch,)), dma((batch,)), dma, dma, dma,
             dma((2 * n_tensor,)), dma((n_seq,)), dma((2 * n_tensor,)), dma((1,)), dma,
             dma((4, n_tensor - 1)), dma((4, n_tensor)), dma((4,)),
             dma((3, PARTS)), dma((3, PARTS)), dma((3, PARTS)), dma((2, PARTS)),
@@ -455,26 +518,23 @@
         compiler_params=pltpu.CompilerParams(
             collective_id=0, has_side_effects=True, vmem_limit_bytes=56 << 20
         ),
-        name="attention_projection",
-    )(attend, gains, begins, weight)
+        name="sections",
+    )(streams, resid, filt, gains, begins, weight)
 
 
 def sums_travel(resid, streams, filt, q_gain, k_gain, out_weight, contig_lengths):
     n_seq, n_tensor = lax.axis_size("seq"), lax.axis_size("tensor")
     section = lax.axis_index("pipe")
-    batch, rows = resid.shape[1:3]
-    tail = streams[0, :, rows - HALO :].astype(jnp.float32)
-    prev = from_behind((tail[:, :, 0] * tail[:, :, 2]).astype(jnp.bfloat16), "seq", 1)
-    hidden, attend = run_hyena(
-        jnp.transpose(streams[0], (0, 2, 1, 3)), resid[0], prev, filt, n_tensor
-    )
+    rows = resid.shape[2]
     gains = jnp.stack([q_gain.reshape(n_tensor, -1), k_gain.reshape(n_tensor, -1)], axis=1)
     gains = jnp.pad(gains, ((0, 0), (0, 6), (0, 0)))
     ends = jnp.cumsum(jnp.where(section == 0, contig_lengths[0], contig_lengths[1]))
     position = jnp.arange(n_seq * rows, dtype=jnp.int32)
     begins = jnp.max(jnp.where(ends[None] <= position[:, None], ends[None], 0), axis=1, keepdims=True)
-    projected = run_attention(attend, gains, begins.astype(jnp.int32), out_weight, n_seq, n_tensor)
-    return jnp.where(section == 0, hidden, projected)[None]
+    return run_sections(
+        jnp.transpose(streams[0], (0, 2, 1, 3)), resid[0], filt, gains, begins.astype(jnp.int32),
+        out_weight, n_seq, n_tensor,
+    )[None]
 
 
 def solution(mesh):

time: 154 us -> 149 us (0.968)
  other arithmetic: 6.02 us -> 2.34 us
  starting transfers between devices: 3.2 us -> 0 us
  Pallas kernels: 139 us -> 142 us
    ppermute x1 -> x0, starting transfers between devices: 3.2 us -> none  [from_behind(): lax.ppermute(value, axis, [(source, source + steps) for source in range(f...]
    broadcast_in_dim x1 -> x0, other arithmetic: 3.14 us -> none  [sums_travel(): return jnp.where(section == 0, hidden, projected)[None]]
    pallas_call x2 -> x1, Pallas kernels: 139 us -> 142 us  [run_sections(): pl.pallas_call(functools.partial(attention_kernel, n_seq, n_tensor, rows)...]
    unnamed x12 -> x1, local copies, waits for them, and re-layouts: 3.77 us -> 3.16 us
  transfers between devices with their start and end apart: 1 -> 0, of which waited for: 1 -> 0; matrix products, arithmetic and copies ran while one was open for 2% -> 0% of each run, Pallas kernels for 0% -> 0%
where the time goes in v2:
time: 149 us; the launch traced here: 148 us
  Pallas kernels  142 us (95%)
  local copies, waits for them, and re-layouts  4.18 us (3%)
  other arithmetic  2.34 us (2%)
    pallas_call x1, Pallas kernels, run_sections(): pl.pallas_call(functools.partial(attention_kernel, n_seq, n_tensor, rows)...  142 us
    unnamed x1, local copies, waits for them, and re-layouts  3.16 us

profile of v2, /device:TPU:13, one launch (start us, length us, event | category | flops | bytes accessed | tf_op | source)
XLA Modules:
  0.0 148.3 jit_solution(3951094543914901127)
XLA Ops:
  0.0 0.8 fusion
  0.8 0.2 reduce-window.8
  0.9 0.1 select_reduce_fusion
  1.0 1.3 select_maximum_fusion.gains_ref
  2.3 1.0 copy.9.begin_ref
  3.4 141.8 %sections.1 = bf16[2,256,2048]{2,1,0:T(8,128)(2,1)} custom-call(bf16[2,3,256,2048]{3,2,1,0:T(8,128)(2,1)} %bitcast.12, bf16[2,256,2048]{2,1,0:T(8,128)(2,1)} %bitcast.13, bf16[7,2048]{1,0:T(8,128)(2,1)} %filt_ref.1, f32[4,8,256]{2,1,0:T(8,128)} %select_maximum_fusion.gains_ref, s32[1024,1]{1,0:T(8,128)} %copy.9.begin_ref, bf16[1024,2048]{1,0:T(8,128)(2,1)} %weight_ref.1), custom_call_target="tpu_custom_call" | custom-call | tf_op jit(solution)/shard_map/sections/pallas_call | solution.py:485
  145.1 3.2 %copy.11 = bf16[1,2,256,2048]{3,2,1,0:T(8,128)(2,1)} copy(bf16[1,2,256,2048]{3,2,1,0:T(8,128)(2,1)} %bitcast.11) | data formatting | bytes 4194304

commit v3 on v2

--- a/solution.py
+++ b/solution.py
@@ -138,7 +138,7 @@
     streams, resid, tail, tail_gated, prev, extended, attend,
     tokens, gains, queries, keys, own_mixed, mixed, weight, partial,
     send_a, recv_a, send_b, recv_b, send_y, recv_y,
-    stream_sem, resid_sem, tail_sem, prev_send, prev_recv,
+    stream_sem, resid_sem, tail_sem, prev_send, prev_recv, hop_send, hop_recv,
     tok_send, tok_recv, gain_send, gain_recv, weight_sem, mix_send, mix_recv, mix_local,
     a_send, a_recv, b_send, b_recv, y_send, y_recv,
 ):
@@ -175,6 +175,14 @@
         return carry
 
     lax.fori_loop(1, world, greet, 0)
+
+    @pl.when(pipe == 0)
+    def _():
+        fetch_tail.wait()
+        tail_gated[...] = (
+            tail[:, 0].astype(jnp.float32) * tail[:, 2].astype(jnp.float32)
+        ).astype(jnp.bfloat16)
+
     pl.semaphore_wait(barrier, world - 1)
 
     def remote(source, target, send_sem, recv_sem, device):
@@ -184,16 +192,15 @@
         )
 
     def to_head_rows(turn):
-        batch, other = 1 - turn // n_tensor, turn % n_tensor
         here = tokens.at[pl.ds(pl.multiple_of(seq * rows, rows), rows)]
-        device = (batch, tensor, other)
-        is_self = (batch == 0) & (seq == tensor) & (other == tensor)
-        return is_self, other, (
-            attend.at[batch, other], here, tok_send.at[turn], tok_recv.at[seq], device
-        ), (gains_ref.at[other], gains, gain_send.at[turn], gain_recv.at[0], device)
+        device = (pipe, tensor, turn)
+        is_self = (seq == tensor) & (turn == tensor)
+        return is_self, (
+            attend.at[pipe, turn], here, tok_send.at[turn], tok_recv.at[seq], device
+        ), (gains_ref.at[turn], gains, gain_send.at[turn], gain_recv.at[0], device)
 
     def send_turn(turn):
-        is_self, other, block, gain = to_head_rows(turn)
+        is_self, block, gain = to_head_rows(turn)
 
         @pl.when(jnp.logical_not(is_self))
         def _():
@@ -212,7 +219,7 @@
             pltpu.make_async_copy(gain[0], gain[1], gain[3]).start()
 
     def wait_turn(turn, carry):
-        is_self, other, block, gain = to_head_rows(turn)
+        is_self, block, gain = to_head_rows(turn)
 
         @pl.when(jnp.logical_not(is_self))
         def _():
@@ -223,6 +230,12 @@
             remote(*gain).wait_send()
 
         return carry
+
+    def hop(turn):
+        return remote(
+            attend.at[1, turn], attend.at[1, turn], hop_send.at[turn], hop_recv.at[turn],
+            (1, seq, tensor),
+        )
 
     def send_prev():
         return remote(tail_gated, prev, prev_send, prev_recv, (0, seq + 1, tensor))
@@ -244,11 +257,6 @@
 
     @pl.when(pipe == 0)
     def _():
-        fetch_tail.wait()
-        tail_gated[...] = (
-            tail[:, 0].astype(jnp.float32) * tail[:, 2].astype(jnp.float32)
-        ).astype(jnp.bfloat16)
-
         @pl.when(seq < n_seq - 1)
         def _():
             send_prev().start()
@@ -285,17 +293,33 @@
                     attend[batch, other, own, head * HD : (head + 1) * HD] = hidden
 
                 hyena(batch, (other * (piece // HD) + head) * 2 * HD, keep)
+
+            @pl.when(batch == 1)
+            def _():
+                hop(other).start()
+
+            @pl.when(batch == 0)
+            def _():
+                send_turn(other)
+
+            return carry
+
+        lax.fori_loop(0, 2 * n_tensor, attended, 0)
+
+    def unattended(turn, carry):
+        batch, other = 1 - turn // n_tensor, turn % n_tensor
+        for head in range(piece // HD):
+            hyena(batch, (other * (piece // HD) + head) * 2 * HD + HD, lambda own, hidden: None)
+        return carry
+
+    @pl.when(pipe == 1)
+    def _():
+        def pass_on(turn, carry):
+            landed(attend.at[1, turn], hop_recv.at[turn])
             send_turn(turn)
             return carry
 
-        def unattended(turn, carry):
-            batch, other = 1 - turn // n_tensor, turn % n_tensor
-            for head in range(piece // HD):
-                hyena(batch, (other * (piece // HD) + head) * 2 * HD + HD, lambda own, hidden: None)
-            return carry
-
-        lax.fori_loop(0, 2 * n_tensor, attended, 0)
-        lax.fori_loop(0, 2 * n_tensor, unattended, 0)
+        lax.fori_loop(0, n_tensor, pass_on, 0)
 
     landed(gains, gain_recv.at[0])
     for source in range(n_seq):
@@ -312,10 +336,10 @@
         order = (3 - step) + (step // 2) * (inner * (2 * step - 5))
         return order + half * (3 - 2 * order)
 
-    def mix_copy(step, hop):
+    def mix_copy(step, stride):
         return remote(
-            own_mixed.at[step], mixed.at[step, :, mine], mix_send.at[step, hop - 1],
-            mix_recv.at[step, tensor], (pipe, seq, lax.rem(tensor + hop, n_tensor)),
+            own_mixed.at[step], mixed.at[step, :, mine], mix_send.at[step, stride - 1],
+            mix_recv.at[step, tensor], (pipe, seq, lax.rem(tensor + stride, n_tensor)),
         )
 
     def attention(step):
@@ -340,8 +364,8 @@
             )
             own_mixed[step, :, lanes] = (result / total).astype(jnp.bfloat16)
         pltpu.make_async_copy(own_mixed.at[step], mixed.at[step, :, mine], mix_local.at[step]).start()
-        for hop in range(1, n_tensor):
-            mix_copy(step, hop).start()
+        for stride in range(1, n_tensor):
+            mix_copy(step, stride).start()
 
     def inward(step, part):
         return remote(
@@ -351,8 +375,8 @@
 
     def project(step):
         pltpu.make_async_copy(own_mixed.at[step], mixed.at[step, :, mine], mix_local.at[step]).wait()
-        for hop in range(1, n_tensor):
-            source = lax.rem(tensor + hop, n_tensor)
+        for stride in range(1, n_tensor):
+            source = lax.rem(tensor + stride, n_tensor)
             lanes = pl.ds(pl.multiple_of(source * piece, piece), piece)
             landed(mixed.at[step, :, lanes], mix_recv.at[step, source])
         width = partial.shape[3]
@@ -385,6 +409,10 @@
 
     lax.fori_loop(0, 5, turn, 0)
 
+    @pl.when(pipe == 0)
+    def _():
+        lax.fori_loop(0, 2 * n_tensor, unattended, 0)
+
     def across(step, part):
         return remote(
             send_a.at[step, part], recv_b.at[step, part], b_send.at[step, part],
@@ -462,15 +490,17 @@
     def _():
         for part in range(PARTS):
             home(part).wait_send()
-        lax.fori_loop(0, 2 * n_tensor, wait_turn, 0)
+        for step in range(n_tensor):
+            hop(step).wait_send()
 
         @pl.when(seq < n_seq - 1)
         def _():
             send_prev().wait_send()
 
+    lax.fori_loop(0, n_tensor, wait_turn, 0)
     for step in range(4):
-        for hop in range(1, n_tensor):
-            mix_copy(step, hop).wait_send()
+        for stride in range(1, n_tensor):
+            mix_copy(step, stride).wait_send()
 
 
 def run_sections(streams, resid, filt, gains, begins, weight, n_seq, n_tensor):
@@ -510,7 +540,8 @@
             pltpu.VMEM((PARTS, rows, part), bf16),
             pltpu.VMEM((PARTS, rows, part), bf16),
             dma((batch,)), dma((batch,)), dma, dma, dma,
-            dma((2 * n_tensor,)), dma((n_seq,)), dma((2 * n_tensor,)), dma((1,)), dma,
+            dma((n_tensor,)), dma((n_tensor,)),
+            dma((n_tensor,)), dma((n_seq,)), dma((n_tensor,)), dma((1,)), dma,
             dma((4, n_tensor - 1)), dma((4, n_tensor)), dma((4,)),
             dma((3, PARTS)), dma((3, PARTS)), dma((3, PARTS)), dma((2, PARTS)),
             dma((PARTS,)), dma((PARTS,)),

time: 149 us -> 128 us (0.86)
  Pallas kernels: 142 us -> 121 us
    pallas_call x1, Pallas kernels: 142 us -> 121 us  [run_sections(): pl.pallas_call(functools.partial(attention_kernel, n_seq, n_tensor, rows)...]
where the time goes in v3:
time: 128 us
  Pallas kernels  121 us (95%)
  local copies, waits for them, and re-layouts  4.18 us (3%)
  other arithmetic  2.34 us (2%)
    pallas_call x1, Pallas kernels, run_sections(): pl.pallas_call(functools.partial(attention_kernel, n_seq, n_tensor, rows)...  121 us
    unnamed x1, local copies, waits for them, and re-layouts  3.16 us

profile of v3, /device:TPU:13, one launch (start us, length us, event | category | flops | bytes accessed | tf_op | source)
XLA Modules:
  0.0 127.7 jit_solution(11719243695251809922)
XLA Ops:
  0.0 0.8 fusion
  0.8 0.2 reduce-window.8
  0.9 0.1 select_reduce_fusion
  1.0 1.3 %select_maximum_fusion.gains_ref = f32[4,8,256]{2,1,0:T(8,128)} fusion(f32[4,1,256]{2,1,0:T(1,128)} %bitcast.15, f32[4,1,256]{2,1,0:T(1,128)} %bitcast.16), kind=kLoop, calls=%fused_computation | loop fusion | flops 32768 | bytes 40960 | tf_op jit(solution)/shard_map/stack | solution.py:560
  2.3 1.0 copy.9.begin_ref
  3.4 121.2 %sections.1 = bf16[2,256,2048]{2,1,0:T(8,128)(2,1)} custom-call(bf16[2,3,256,2048]{3,2,1,0:T(8,128)(2,1)} %bitcast.12, bf16[2,256,2048]{2,1,0:T(8,128)(2,1)} %bitcast.13, bf16[7,2048]{1,0:T(8,128)(2,1)} %filt_ref.1, f32[4,8,256]{2,1,0:T(8,128)} %select_maximum_fusion.gains_ref, s32[1024,1]{1,0:T(8,128)} %copy.9.begin_ref, bf16[1024,2048]{1,0:T(8,128)(2,1)} %weight_ref.1), custom_call_target="tpu_custom_call" | custom-call | tf_op jit(solution)/shard_map/sections/pallas_call | solution.py:515
  124.6 3.2 %copy.11 = bf16[1,2,256,2048]{3,2,1,0:T(8,128)(2,1)} copy(bf16[1,2,256,2048]{3,2,1,0:T(8,128)(2,1)} %bitcast.11) | data formatting | bytes 4194304

commit v4 on v3

--- a/solution.py
+++ b/solution.py
@@ -134,7 +134,7 @@
 
 
 def attention_kernel(
-    n_seq, n_tensor, rows, streams_ref, resid_ref, filt_ref, gains_ref, begin_ref, weight_ref, out_ref,
+    n_seq, n_tensor, rows, streams_ref, resid_ref, filt_ref, gains_ref, lengths_ref, weight_ref, out_ref,
     streams, resid, tail, tail_gated, prev, extended, attend,
     tokens, gains, queries, keys, own_mixed, mixed, weight, partial,
     send_a, recv_a, send_b, recv_b, send_y, recv_y,
@@ -348,7 +348,12 @@
         low = pl.multiple_of((chunk // 3) * rows, rows)
         position = first + lax.broadcasted_iota(jnp.int32, (rows, window), 0)
         key_position = low + lax.broadcasted_iota(jnp.int32, (rows, window), 1)
-        visible = (key_position >= begin_ref[pl.ds(first, rows)]) & (key_position <= position)
+        token = first + lax.broadcasted_iota(jnp.int32, (rows, 1), 0)
+        begin, end = jnp.zeros((rows, 1), jnp.int32), 0
+        for contig in range(lengths_ref.shape[1]):
+            end = end + lengths_ref[pipe, contig]
+            begin = jnp.where(token >= end, end, begin)
+        visible = (key_position >= begin) & (key_position <= position)
         for head in range(piece // HD):
             lanes = slice(head * HD, (head + 1) * HD)
             scores = lax.dot_general(
@@ -503,7 +508,7 @@
             mix_copy(step, stride).wait_send()
 
 
-def run_sections(streams, resid, filt, gains, begins, weight, n_seq, n_tensor):
+def run_sections(streams, resid, filt, gains, lengths, weight, n_seq, n_tensor):
     batch, rows = resid.shape[:2]
     piece = gains.shape[2]
     depth, width = weight.shape
@@ -514,7 +519,7 @@
     anywhere, vmem = pl.BlockSpec(memory_space=pl.ANY), pl.BlockSpec(memory_space=pltpu.VMEM)
     return pl.pallas_call(
         functools.partial(attention_kernel, n_seq, n_tensor, rows),
-        in_specs=[anywhere, anywhere, vmem, anywhere, vmem, anywhere],
+        in_specs=[anywhere, anywhere, vmem, anywhere, pl.BlockSpec(memory_space=pltpu.SMEM), anywhere],
         out_specs=vmem,
         out_shape=jax.ShapeDtypeStruct((batch, rows, width), bf16),
         scratch_shapes=[
@@ -550,20 +555,15 @@
             collective_id=0, has_side_effects=True, vmem_limit_bytes=56 << 20
         ),
         name="sections",
-    )(streams, resid, filt, gains, begins, weight)
+    )(streams, resid, filt, gains, lengths, weight)
 
 
 def sums_travel(resid, streams, filt, q_gain, k_gain, out_weight, contig_lengths):
     n_seq, n_tensor = lax.axis_size("seq"), lax.axis_size("tensor")
-    section = lax.axis_index("pipe")
-    rows = resid.shape[2]
     gains = jnp.stack([q_gain.reshape(n_tensor, -1), k_gain.reshape(n_tensor, -1)], axis=1)
     gains = jnp.pad(gains, ((0, 0), (0, 6), (0, 0)))
-    ends = jnp.cumsum(jnp.where(section == 0, contig_lengths[0], contig_lengths[1]))
-    position = jnp.arange(n_seq * rows, dtype=jnp.int32)
-    begins = jnp.max(jnp.where(ends[None] <= position[:, None], ends[None], 0), axis=1, keepdims=True)
     return run_sections(
-        jnp.transpose(streams[0], (0, 2, 1, 3)), resid[0], filt, gains, begins.astype(jnp.int32),
+        jnp.transpose(streams[0], (0, 2, 1, 3)), resid[0], filt, gains, contig_lengths,
         out_weight, n_seq, n_tensor,
     )[None]
 

time: 128 us -> 126 us (0.984)
  no operation moved by 1% of the time
where the time goes in v4:
time: 126 us; the launch traced here: 125 us
  Pallas kernels  121 us (96%)
  local copies, waits for them, and re-layouts  3.16 us (3%)
  other arithmetic  1.33 us (1%)
    pallas_call x1, Pallas kernels, run_sections(): pl.pallas_call(functools.partial(attention_kernel, n_seq, n_tensor, rows)...  121 us
    unnamed x1, local copies, waits for them, and re-layouts  3.16 us

profile of v4, /device:TPU:13, one launch (start us, length us, event | category | flops | bytes accessed | tf_op | source)
XLA Modules:
  0.0 125.5 jit_solution(10530456116837086787)
XLA Ops:
  0.0 1.3 %select_maximum_fusion.gains_ref = f32[4,8,256]{2,1,0:T(8,128)} fusion(f32[4,1,256]{2,1,0:T(1,128)} %bitcast.10, f32[4,1,256]{2,1,0:T(1,128)} %bitcast.11), kind=kLoop, calls=%fused_computation | loop fusion | flops 32768 | bytes 40960 | tf_op jit(solution)/shard_map/stack | solution.py:563
  1.3 121.0 %sections.1 = bf16[2,256,2048]{2,1,0:T(8,128)(2,1)} custom-call(bf16[2,3,256,2048]{3,2,1,0:T(8,128)(2,1)} %bitcast.8, bf16[2,256,2048]{2,1,0:T(8,128)(2,1)} %bitcast.9, bf16[7,2048]{1,0:T(8,128)(2,1)} %filt_ref.1, f32[4,8,256]{2,1,0:T(8,128)} %select_maximum_fusion.gains_ref, s32[2,4]{1,0:T(2,128)} %lengths_ref.1, bf16[1024,2048]{1,0:T(8,128)(2,1)} %weight_ref.1), custom_call_target="tpu_custom_call" | custom-call | tf_op jit(solution)/shard_map/sections/pallas_call | solution.py:520
  122.3 3.2 %copy.9 = bf16[1,2,256,2048]{3,2,1,0:T(8,128)(2,1)} copy(bf16[1,2,256,2048]{3,2,1,0:T(8,128)(2,1)} %bitcast.7) | data formatting | bytes 4194304
